TPU v7x, 256 devices: a whole 4x4x8 slice. The times are simulated.
256 devices in a mesh: dp: 4 (over z_lo), space: 8 (over x, z_hi), tensor: 8 (over y, core).
Axes of the slice: x: 4, y: 4, z: 8 (z_hi: 2, z_lo: 4; z = z_hi * 4 + z_lo), core: 2. Of those that a mesh axis runs over, the one named last changes fastest.
Arguments:
- features: bfloat16 [4, 128, 64, 1024], P('dp', ('space', 'tensor')), may hold values from -6 to 6
- kernel: bfloat16 [3, 3, 1024, 1024], P(None, None, 'tensor'), may hold values from -0.0625 to 0.0625
- embedding: float32 [1000, 1024], P(None, 'tensor'), may hold values from -6 to 6
- labels: int32 [4], P('dp'), may hold values from 0 to 999
Outputs:
- weight_grad: float32 [3, 3, 1024, 1024], P(None, None, 'tensor')
- embed_grad: float32 [1000, 1024], P(None, 'tensor')
All inputs are finite; a program needn't handle non-finite values.
Results may differ from a plain program's by a relative error of at most 0.00033.
Values may be sent and summed in bfloat16 or wider, within the bound.
No kernel may reach another device: no remote copies, remote signals or barrier semaphores. Data moves between devices by JAX's collectives and lax.ppermute only.
A program may use at most 64 MiB of HBM per device.

v0:
```python
import math
import jax
import jax.numpy as jnp
from jax import lax
from jax.sharding import PartitionSpec as P

r1_factor = 1000.0


def padded_2(block, sides, width):
    for axis, dim in sides:
        count = lax.axis_size(axis)
        forward = [(i, i + 1) for i in range(count - 1)]
        backward = [(target, source) for source, target in forward]
        low = lax.ppermute(
            lax.slice_in_dim(block, block.shape[dim] - width, None, axis=dim), axis, forward
        )
        high = lax.ppermute(lax.slice_in_dim(block, 0, width, axis=dim), axis, backward)
        block = jnp.concatenate([low, block, high], axis=dim)
    return block


def conv_valid(padded, kern):
    return lax.conv_general_dilated(
        padded,
        kern,
        (1, 1),
        "VALID",
        dimension_numbers=("NHWC", "HWIO", "NHWC"),
        preferred_element_type=jnp.float32,
    )


def pad_cols(field):
    return jnp.pad(field, ((0, 0), (0, 0), (1, 1), (0, 0)))


def taps_of(padded, grad):
    row_count = grad.shape[1]
    col_count = grad.shape[2]
    flat_grad = grad.reshape(-1, grad.shape[3])
    outer = []
    for tap_row in range(3):
        inner = []
        for tap_col in range(3):
            window = padded[
                :, tap_row : tap_row + row_count, tap_col : tap_col + col_count, :
            ].reshape(-1, padded.shape[3])
            inner.append(
                lax.dot_general(
                    window, flat_grad, (((0,), (0,)), ((), ())), preferred_element_type=jnp.float32
                )
            )
        outer.append(jnp.stack(inner))
    return jnp.stack(outer)


def forward_conv(padded, kernel_cols):
    whole = lax.all_gather(padded, "tensor", axis=3, tiled=True)
    return conv_valid(whole, kernel_cols)


def body(features, kernel, embedding, labels):
    tensor_count = lax.axis_size("tensor")
    space_count = lax.axis_size("space")
    image_total = features.shape[0] * lax.axis_size("dp")
    col_count = features.shape[2]
    chan_total = features.shape[3]
    height = features.shape[1] * tensor_count * space_count
    scale = 1.0 / math.sqrt(height * col_count * chan_total)
    gweight = r1_factor / image_total
    local_maps = lax.all_to_all(features, "tensor", split_axis=3, concat_axis=1, tiled=True)
    x_pad = pad_cols(padded_2(local_maps, (("space", 1),), 1))
    kernel_cols = lax.all_to_all(kernel, "tensor", split_axis=3, concat_axis=2, tiled=True)
    hidden = forward_conv(x_pad, kernel_cols)
    class_count = embedding.shape[0]
    onehot = (labels[:, None] == jnp.arange(class_count, dtype=jnp.int32)[None, :]).astype(
        jnp.float32
    )
    embed_rows = jnp.dot(onehot, embedding, precision=lax.Precision.HIGHEST)
    embed_four = embed_rows[:, None, None, :]
    sig = jax.nn.sigmoid(hidden)
    act = hidden * sig
    slope = sig * (1.0 + hidden * (1.0 - sig))
    curve = sig * (1.0 - sig) * (2.0 + hidden * (1.0 - 2.0 * sig))
    score = lax.psum(scale * jnp.sum(act * embed_four, axis=(1, 2, 3)), ("space", "tensor"))
    coeff = -jax.nn.sigmoid(-score) / image_total
    grad_hidden = (embed_four * slope * scale).astype(jnp.bfloat16)
    gh_pad = pad_cols(padded_2(grad_hidden, (("space", 1),), 1))
    flipped = jnp.transpose(kernel[::-1, ::-1], (0, 1, 3, 2))
    gh_whole = lax.all_gather(gh_pad, "tensor", axis=3, tiled=True)
    grad_input = conv_valid(gh_whole, flipped).astype(jnp.bfloat16)
    gx_pad = pad_cols(padded_2(grad_input, (("space", 1),), 1))
    direct = taps_of(gx_pad, gh_whole[:, 1:-1, 1:-1, :])
    second = forward_conv(gx_pad, kernel_cols)
    pre = (
        coeff[:, None, None, None] * embed_four * slope * scale
        + gweight * second * embed_four * curve * scale
    ).astype(jnp.bfloat16)
    adversarial = taps_of(x_pad, lax.all_gather(pre, "tensor", axis=3, tiled=True))
    wgrad = adversarial + gweight * direct
    per_image = coeff[:, None] * scale * jnp.sum(act, axis=(1, 2)) + gweight * scale * jnp.sum(
        second * slope, axis=(1, 2)
    )
    egrad = jnp.dot(onehot.T, per_image, precision=lax.Precision.HIGHEST)
    wtotal, etotal = lax.psum((wgrad, egrad), ("dp", "space"))
    return (wtotal, etotal)


def solution(mesh):
    placed = (
        P("dp", ("space", "tensor"), None, None),
        P(None, None, "tensor", None),
        P(None, "tensor"),
        P("dp"),
    )
    return jax.shard_map(
        body,
        mesh=mesh,
        in_specs=placed,
        out_specs=(P(None, None, "tensor", None), P(None, "tensor")),
        check_vma=False,
    )
```

profile of v0, /device:TPU:1, one launch (start us, length us, event | category | flops | bytes accessed | tf_op | source)
XLA Modules:
  0.0 670.4 jit_solution(11944661111741566787)
XLA Ops:
  7.2 2.1 copy.31
  9.3 1.4 reshape.249
  10.8 12.3 %all_to_all.36 = bf16[8,2,8192]{2,1,0:T(2,128)(2,1)S(1)} all-to-all(bf16[8,2,8192]{2,1,0:T(2,128)(2,1)S(1)} %reshape.249), channel_id=1, replica_groups=mesh['dp'=4,'space'=8,'tensor'=8] {'tensor'}, dimensions={0} | all-to-all | bytes 524288 | tf_op jit(solution)/shard_map/all_to_all | solution.py:72
  23.0 1.2 reshape.250
  24.2 1.2 copy.32
  25.5 1.3 collective-permute-start.1
  26.8 9.4 %collective-permute-start = (bf16[1,1,64,128]{3,2,1,0:T(8,128)(2,1)S(1)}, bf16[1,1,64,128]{3,2,1,0:T(8,128)(2,1)S(1)}, u32[]{:S(2)}, u32[]{:S(2)}) collective-permute-start(bf16[1,1,64,128]{3,2,1,0:T(8,128)(2,1)S(1)} %get-tuple-element.11), channel_id=1, source_target_pairs={{0,8},{8,16},{16,24},{24,32},{32,40},{40,48},{48,56},{1,9},{9,17},... | collective-permute-start | bytes 49160 | tf_op jit(solution)/shard_map/ppermute | solution.py:15
  36.2 0.8 collective-permute-done
  37.1 0.8 select_maximum_fusion.4
  37.9 3.6 copy.36
  41.5 6.2 all-to-all-start.1
  48.7 47.4 %all-to-all-done.1 = bf16[3,3,128,1024]{2,1,0,3:T(4,128)(2,1)} async-done(((bf16[3,3,128,1024]{2,1,0,3:T(4,128)(2,1)}), bf16[3,3,128,1024]{2,1,0,3:T(4,128)(2,1)}, u32[]{:S(2)}, u32[]{:S(2)}) %all-to-all-start.1) | async-done | bytes 2359328 | tf_op jit(solution)/shard_map/all_to_all | solution.py:74
  96.1 5.6 copy.37
  101.7 3.2 copy.60
  105.5 1.5 copy.35
  107.2 6.5 multiply_convert_fusion
  113.8 1.3 collective-permute-start.3
  115.1 9.5 %collective-permute-start.2 = (bf16[1,1,64,128]{3,2,1,0:T(8,128)(2,1)S(1)}, bf16[1,1,64,128]{3,2,1,0:T(8,128)(2,1)S(1)}, u32[]{:S(2)}, u32[]{:S(2)}) collective-permute-start(bf16[1,1,64,128]{3,2,1,0:T(8,128)(2,1)S(1)} %slice.123), channel_id=1, source_target_pairs={{0,8},{8,16},{16,24},{24,32},{32,40},{40,48},{48,56},{1,9},{9,17},... | collective-permute-start | bytes 49160 | tf_op jit(solution)/shard_map/ppermute | solution.py:15
  125.1 0.8 select_maximum_fusion.2
  126.0 39.5 %all-gather.8.cloned.1.call-done = bf16[1,18,66,1024]{3,2,1,0:T(8,128)(2,1)} async-done(((bf16[1,18,66,128]{3,2,1,0:T(8,128)(2,1)}), bf16[1,18,66,1024]{3,2,1,0:T(8,128)(2,1)}) %all-gather.8.cloned.1.call-update) | async-done | bytes 2433040 | tf_op jit(solution)/shard_map/all_gather | solution.py:91
  165.5 3.2 copy.61
  169.2 1.5 copy.44
  170.8 5.7 fusion.81
  176.6 1.3 collective-permute-start.5
  178.0 8.0 %collective-permute-start.4 = (bf16[1,1,64,128]{3,2,1,0:T(8,128)(2,1)S(1)}, bf16[1,1,64,128]{3,2,1,0:T(8,128)(2,1)S(1)}, u32[]{:S(2)}, u32[]{:S(2)}) collective-permute-start(bf16[1,1,64,128]{3,2,1,0:T(8,128)(2,1)S(1)} %slice.129), channel_id=1, source_target_pairs={{0,8},{8,16},{16,24},{24,32},{32,40},{40,48},{48,56},{1,9},{9,17},... | collective-permute-start | bytes 49160 | tf_op jit(solution)/shard_map/ppermute | solution.py:15
  186.9 0.8 select_maximum_fusion
  188.0 36.1 %all-gather.10.cloned.1.call-done = bf16[1,18,66,1024]{3,2,1,0:T(8,128)(2,1)} async-done(((bf16[1,18,66,128]{3,2,1,0:T(8,128)(2,1)}), bf16[1,18,66,1024]{3,2,1,0:T(8,128)(2,1)}) %all-gather.10.cloned.1.call-update) | async-done | bytes 2433040 | tf_op jit(solution)/shard_map/all_gather | solution.py:59
  224.0 3.2 copy.62
  227.8 1.5 copy.51
  229.6 7.2 %select_reduce_fusion.2 = (f32[128]{0:T(128)S(1)}, f32[128]{0:T(128)S(1)}, f32[]{:T(128)}, f32[16,8,9,128]{3,1,2,0:T(8,128)}) fusion(pred[8,9]{0,1:T(8,128)(4,1)S(1)} %copy-done.17, f32[16,8,9,128]{3,1,2,0:T(8,128)S(1)} %copy-done.15, f32[128]{0:T(128)S(1)} %convolution_bitcast_fusion.9, bf16[3,3,1024,128]{3,2,1,0:T(8,128)(2,1)S(1)} %bitcast.242, ...), kind=kOutput, calls=%fused_computation.90 | convolution fusion | flops 2730147840 | bytes 6710860 | tf_op jit(solution)/shard_map/conv_general_dilated | solution.py:24
  237.5 201.6 %psum.21 = f32[1]{0:T(128)} all-reduce(f32[1]{0:T(128)} %bitcast.13), channel_id=1, replica_groups=mesh['dp'=4,'space'=8,'tensor'=8] {'space','tensor'}, use_global_device_ids=true, to_apply=%region_1.2 | all-reduce | flops 1 | bytes 8 | tf_op jit(solution)/shard_map/psum | solution.py:86
  439.8 1.7 fusion.91
  442.6 1.8 convolution_bitcast_fusion.4
  444.4 1.8 convolution_bitcast_fusion.1
  446.2 0.8 convolution_bitcast_fusion
  448.1 1.6 copy-done.7
  449.6 0.8 convolution_bitcast_fusion.7
  450.4 0.8 convolution_bitcast_fusion.6
  451.3 0.8 convolution_bitcast_fusion.8
  452.1 0.8 convolution_bitcast_fusion.3
  453.7 1.9 maximum_bitcast_fusion.3
  455.6 1.0 broadcast_multiply_fusion
  456.6 16.8 %all-gather.12.cloned.1.call-done = bf16[16,1,64,1024]{3,2,0,1:T(8,128)(2,1)} async-done(((bf16[16,1,64,128]{3,2,0,1:T(8,128)(2,1)}), bf16[16,1,64,1024]{3,2,0,1:T(8,128)(2,1)}) %all-gather.12.cloned.1.call-update) | async-done | bytes 2097168 | tf_op jit(solution)/shard_map/all_gather | solution.py:100
  473.4 2.2 fusion.69
  480.0 1.1 copy-done.4
  481.6 2.7 maximum_add_fusion
  484.3 173.2 %all-reduce.6.cloned.1.call-done = (f32[3,3,128,1024]{3,2,1,0:T(8,128)}, f32[1000,128]{1,0:T(8,128)}) async-done(((f32[3,3,128,1024]{3,2,1,0:T(8,128)}, f32[1000,128]{1,0:T(8,128)}), (f32[3,3,128,1024]{3,2,1,0:T(8,128)}, f32[1000,128]{1,0:T(8,128)})) %all-reduce.6.cloned.1.call-update) | async-done | bytes 5230608 | tf_op jit(solution)/shard_map/psum | solution.py:106
  657.5 5.3 copy.74
  (100 shorter events, 12.8 us)
Async XLA Ops:
  7.2 41.3 %copy-start = (f32[1000,128]{1,0:T(8,128)S(1)}, f32[1000,128]{1,0:T(8,128)}, u32[]{:S(2)}) copy-start(f32[1000,128]{1,0:T(8,128)} %param.6) | copy-start | bytes 1536004
  7.2 30.7 %copy-start.8 = (bf16[3,3,128,1024]{3,2,1,0:T(8,128)(2,1)S(1)}, bf16[3,3,128,1024]{3,2,1,0:T(8,128)(2,1)}, u32[]{:S(2)}) copy-start(bf16[3,3,128,1024]{3,2,1,0:T(8,128)(2,1)} %param.5) | copy-start | bytes 7077892
  7.2 94.5 %all-gather.6.cloned.1.call-start = ((), (), s32[]{:S(2)}) async-start(), calls=%async_computation.2 | async-start | bytes 2985984 | tf_op jit(solution)/shard_map/all_gather | solution.py:59
  25.5 10.8 %collective-permute-start.1 = (bf16[1,1,64,128]{3,2,1,0:T(8,128)(2,1)S(1)}, bf16[1,1,64,128]{3,2,1,0:T(8,128)(2,1)S(1)}, u32[]{:S(2)}, u32[]{:S(2)}) collective-permute-start(bf16[1,1,64,128]{3,2,1,0:T(8,128)(2,1)S(1)} %get-tuple-element.12), channel_id=1, source_target_pairs={{8,0},{16,8},{24,16},{32,24},{40,32},{48,40},{56,48},{9,1},{17,9},... | collective-permute-start | bytes 49160 | tf_op jit(solution)/shard_map/ppermute | solution.py:18
  26.8 10.3 %collective-permute-start = (bf16[1,1,64,128]{3,2,1,0:T(8,128)(2,1)S(1)}, bf16[1,1,64,128]{3,2,1,0:T(8,128)(2,1)S(1)}, u32[]{:S(2)}, u32[]{:S(2)}) collective-permute-start(bf16[1,1,64,128]{3,2,1,0:T(8,128)(2,1)S(1)} %get-tuple-element.11), channel_id=1, source_target_pairs={{0,8},{8,16},{16,24},{24,32},{32,40},{40,48},{48,56},{1,9},{9,17},... | collective-permute-start | bytes 49160 | tf_op jit(solution)/shard_map/ppermute | solution.py:15
  41.5 54.6 %all-to-all-start.1 = ((bf16[3,3,128,1024]{2,1,0,3:T(4,128)(2,1)}), bf16[3,3,128,1024]{2,1,0,3:T(4,128)(2,1)}, u32[]{:S(2)}, u32[]{:S(2)}) async-start(bf16[3,3,128,1024]{2,1,0,3:T(4,128)(2,1)} %copy.36), calls=%async_computation.1 | async-start | bytes 6291456 | tf_op jit(solution)/shard_map/all_to_all | solution.py:74
  47.8 117.7 %all-gather.8.cloned.1.call-start = ((), (), s32[]{:S(2)}) async-start(), calls=%async_computation.3 | async-start | bytes 2985984 | tf_op jit(solution)/shard_map/all_gather | solution.py:91
  105.5 1.7 copy-start.9
  105.5 1.7 copy-start.17
  113.8 11.1 %collective-permute-start.3 = (bf16[1,1,64,128]{3,2,1,0:T(8,128)(2,1)S(1)}, bf16[1,1,64,128]{3,2,1,0:T(8,128)(2,1)S(1)}, u32[]{:S(2)}, u32[]{:S(2)}) collective-permute-start(bf16[1,1,64,128]{3,2,1,0:T(8,128)(2,1)S(1)} %slice.126), channel_id=1, source_target_pairs={{8,0},{16,8},{24,16},{32,24},{40,32},{48,40},{56,48},{9,1},{17,9},... | collective-permute-start | bytes 49160 | tf_op jit(solution)/shard_map/ppermute | solution.py:18
  115.1 9.9 %collective-permute-start.2 = (bf16[1,1,64,128]{3,2,1,0:T(8,128)(2,1)S(1)}, bf16[1,1,64,128]{3,2,1,0:T(8,128)(2,1)S(1)}, u32[]{:S(2)}, u32[]{:S(2)}) collective-permute-start(bf16[1,1,64,128]{3,2,1,0:T(8,128)(2,1)S(1)} %slice.123), channel_id=1, source_target_pairs={{0,8},{8,16},{16,24},{24,32},{32,40},{40,48},{48,56},{1,9},{9,17},... | collective-permute-start | bytes 49160 | tf_op jit(solution)/shard_map/ppermute | solution.py:15
  125.9 98.1 %all-gather.10.cloned.1.call-start = ((), (), s32[]{:S(2)}) async-start(), calls=%async_computation.4 | async-start | bytes 2985984 | tf_op jit(solution)/shard_map/all_gather | solution.py:59
  176.6 10.2 %collective-permute-start.5 = (bf16[1,1,64,128]{3,2,1,0:T(8,128)(2,1)S(1)}, bf16[1,1,64,128]{3,2,1,0:T(8,128)(2,1)S(1)}, u32[]{:S(2)}, u32[]{:S(2)}) collective-permute-start(bf16[1,1,64,128]{3,2,1,0:T(8,128)(2,1)S(1)} %slice.132), channel_id=1, source_target_pairs={{8,0},{16,8},{24,16},{32,24},{40,32},{48,40},{56,48},{9,1},{17,9},... | collective-permute-start | bytes 49160 | tf_op jit(solution)/shard_map/ppermute | solution.py:18
  178.0 8.9 %collective-permute-start.4 = (bf16[1,1,64,128]{3,2,1,0:T(8,128)(2,1)S(1)}, bf16[1,1,64,128]{3,2,1,0:T(8,128)(2,1)S(1)}, u32[]{:S(2)}, u32[]{:S(2)}) collective-permute-start(bf16[1,1,64,128]{3,2,1,0:T(8,128)(2,1)S(1)} %slice.129), channel_id=1, source_target_pairs={{0,8},{8,16},{16,24},{24,32},{32,40},{40,48},{48,56},{1,9},{9,17},... | collective-permute-start | bytes 49160 | tf_op jit(solution)/shard_map/ppermute | solution.py:15
  186.0 0.7 copy-start.14
  186.8 40.4 %copy-start.12 = (bf16[16,1,64,128]{3,2,0,1:T(8,128)(2,1)}, bf16[16,1,64,128]{3,2,0,1:T(8,128)(2,1)S(1)}, u32[]{:S(2)}) copy-start(bf16[16,1,64,128]{3,2,0,1:T(8,128)(2,1)S(1)} %copy.70) | copy-start | bytes 786436
  187.7 285.7 %all-gather.12.cloned.1.call-start = ((), (), s32[]{:S(2)}) async-start(), calls=%async_computation.5 | async-start | bytes 2359296 | tf_op jit(solution)/shard_map/all_gather | solution.py:100
  227.8 1.7 copy-start.10
  227.8 1.8 copy-start.15
  236.8 205.8 %copy-start.6 = (bf16[1,18,66,1024]{3,2,1,0:T(8,128)(2,1)S(1)}, bf16[1,18,66,1024]{3,2,1,0:T(8,128)(2,1)}, u32[]{:S(2)}) copy-start(bf16[1,18,66,1024]{3,2,1,0:T(8,128)(2,1)} %all-gather.8.cloned.1.call-done) | copy-start | bytes 7299076
  442.4 215.2 %all-reduce.6.cloned.1.call-start = ((), (), s32[]{:S(2)}) async-start(), calls=%async_computation.6 | async-start | bytes 10461184 | tf_op jit(solution)/shard_map/psum | solution.py:106
  444.4 1.8 copy-start.11
  447.9 1.8 copy-start.7
  447.9 1.7 copy-start.13
  453.7 19.7 %copy-start.3 = (bf16[1,18,66,128]{3,2,1,0:T(8,128)(2,1)S(1)}, bf16[1,18,66,128]{3,2,1,0:T(8,128)(2,1)}, u32[]{:S(2)}) copy-start(bf16[1,18,66,128]{3,2,1,0:T(8,128)(2,1)} %select_maximum_fusion.4) | copy-start | bytes 912388
  473.4 2.2 copy-start.2
  479.7 1.4 copy-start.4
  479.7 1.9 copy-start.5
  657.5 5.3 copy-start.16
  657.5 6.1 copy-start.1
Sparse Core Ops, SparseCore 0:
  38.0 50.9 all-gather.5
  126.0 39.3 all-gather.7
  187.8 36.1 all-gather.9
  442.5 30.9 all-gather.11
  484.4 173.0 all-reduce.5
where the time goes:
time: 679 us; the launch traced here: 670 us
  waiting for transfers between devices  314 us (46%)
  blocking collectives  214 us (32%)
  local copies, waits for them, and re-layouts  42.6 us (6%)
  starting transfers between devices  37.6 us (6%)
  matrix products  35 us (5%)
  between operations  16.7 us (2%)
  other arithmetic  10.4 us (2%)
    psum x1, blocking collectives, body(): lax.psum(scale * jnp.sum(act * embed_four, axis=(1, 2, 3)), ('space', 'te...  202 us
    psum x1, waiting for transfers between devices, body(): wtotal, etotal = lax.psum((wgrad, egrad), ('dp', 'space'))  173 us
    all_to_all x1, waiting for transfers between devices, body(): lax.all_to_all(kernel, 'tensor', split_axis=3, concat_axis=2, tiled=True)  47.4 us
    all_gather x1, waiting for transfers between devices, body(): gh_whole = lax.all_gather(gh_pad, 'tensor', axis=3, tiled=True)  39.5 us
    all_gather x2, waiting for transfers between devices, forward_conv(): whole = lax.all_gather(padded, 'tensor', axis=3, tiled=True)  36.1 us
    unnamed x48, local copies, waits for them, and re-layouts  28.9 us
    ppermute x3, starting transfers between devices, padded_2(): lax.ppermute(lax.slice_in_dim(block, block.shape[dim] - width, None, axis...  27 us
    conv_general_dilated x3, matrix products, conv_valid(): lax.conv_general_dilated(padded, kern, (1, 1), 'VALID', dimension_numbers...  19.5 us
  transfers between devices with their start and end apart: 12, of which 7 were waited for; matrix products, arithmetic and copies ran while one was open for 3% of the time, Pallas kernels for 0%

commit v1 on v0

--- a/solution.py
+++ b/solution.py
@@ -5,6 +5,22 @@
 from jax.sharding import PartitionSpec as P
 
 r1_factor = 1000.0
+
+
+def pairwise_exchange(value, axis, split, join):
+    ways, here = (lax.axis_size(axis), lax.axis_index(axis))
+    width = value.shape[split] // ways
+    dims = list(value.shape)
+    dims[split] = width
+    height = dims[join]
+    dims[join] = height * ways
+    full = jnp.zeros(dims, value.dtype)
+    for mask in range(ways):
+        part = lax.dynamic_slice_in_dim(value, (here ^ mask) * width, width, axis=split)
+        if mask:
+            part = lax.ppermute(part, axis, [(d, d ^ mask) for d in range(ways)])
+        full = lax.dynamic_update_slice_in_dim(full, part, (here ^ mask) * height, axis=join)
+    return full
 
 
 def padded_2(block, sides, width):
@@ -71,7 +87,7 @@
     gweight = r1_factor / image_total
     local_maps = lax.all_to_all(features, "tensor", split_axis=3, concat_axis=1, tiled=True)
     x_pad = pad_cols(padded_2(local_maps, (("space", 1),), 1))
-    kernel_cols = lax.all_to_all(kernel, "tensor", split_axis=3, concat_axis=2, tiled=True)
+    kernel_cols = pairwise_exchange(kernel, "tensor", 3, 2)
     hidden = forward_conv(x_pad, kernel_cols)
     class_count = embedding.shape[0]
     onehot = (labels[:, None] == jnp.arange(class_count, dtype=jnp.int32)[None, :]).astype(

time: 679 us -> 661 us (0.973)
  local copies, waits for them, and re-layouts: 42.6 us -> 32.2 us
  waiting for transfers between devices: 314 us -> 305 us
    all_to_all x1 -> x0, waiting for transfers between devices: 47.4 us -> none  [body(): lax.all_to_all(kernel, 'tensor', split_axis=3, concat_axis=2, tiled=True)]
    ppermute x0 -> x7, waiting for transfers between devices: none -> 32.7 us  [pairwise_exchange(): part = lax.ppermute(part, axis, [(d, d ^ mask) for d in range(ways)])]
    ppermute x0 -> x7, starting transfers between devices: none -> 10.5 us  [pairwise_exchange(): part = lax.ppermute(part, axis, [(d, d ^ mask) for d in range(ways)])]
    unnamed x48 -> x43, local copies, waits for them, and re-layouts: 28.9 us -> 22.5 us
  transfers between devices with their start and end apart: 12 -> 18, of which waited for: 7 -> 12; matrix products, arithmetic and copies ran while one was open for 3% -> 2% of each run, Pallas kernels for 0% -> 0%
where the time goes in v1:
time: 661 us; the launch traced here: 655 us
  waiting for transfers between devices  305 us (46%)
  blocking collectives  214 us (32%)
  starting transfers between devices  41.4 us (6%)
  matrix products  35 us (5%)
  local copies, waits for them, and re-layouts  32.2 us (5%)
  between operations  17.1 us (3%)
  other arithmetic  10.4 us (2%)
    psum x1, blocking collectives, body(): lax.psum(scale * jnp.sum(act * embed_four, axis=(1, 2, 3)), ('space', 'te...  202 us
    psum x1, waiting for transfers between devices, body(): wtotal, etotal = lax.psum((wgrad, egrad), ('dp', 'space'))  173 us
    all_gather x2, waiting for transfers between devices, forward_conv(): whole = lax.all_gather(padded, 'tensor', axis=3, tiled=True)  42.4 us
    all_gather x1, waiting for transfers between devices, body(): gh_whole = lax.all_gather(gh_pad, 'tensor', axis=3, tiled=True)  38.6 us
    ppermute x7, waiting for transfers between devices, pairwise_exchange(): part = lax.ppermute(part, axis, [(d, d ^ mask) for d in range(ways)])  32.7 us
    ppermute x3, starting transfers between devices, padded_2(): lax.ppermute(lax.slice_in_dim(block, block.shape[dim] - width, None, axis...  26.1 us
    unnamed x43, local copies, waits for them, and re-layouts  22.5 us
    conv_general_dilated x3, matrix products, conv_valid(): lax.conv_general_dilated(padded, kern, (1, 1), 'VALID', dimension_numbers...  19.5 us
  transfers between devices with their start and end apart: 18, of which 12 were waited for; matrix products, arithmetic and copies ran while one was open for 2% of the time, Pallas kernels for 0%

profile of v1, /device:TPU:1, one launch (start us, length us, event | category | flops | bytes accessed | tf_op | source)
XLA Modules:
  0.0 655.3 jit_solution(9800697105551223320)
XLA Ops:
  7.2 1.3 copy.29
  8.9 12.3 %all_to_all.18 = bf16[8,2,8192]{2,1,0:T(2,128)(2,1)S(1)} all-to-all(bf16[8,2,8192]{2,1,0:T(2,128)(2,1)S(1)} %reshape.249), channel_id=1, replica_groups=mesh['dp'=4,'space'=8,'tensor'=8] {'tensor'}, dimensions={0} | all-to-all | bytes 524288 | tf_op jit(solution)/shard_map/all_to_all | solution.py:88
  21.9 1.3 collective-permute-start.1
  23.2 9.4 %collective-permute-start = (bf16[1,1,64,128]{3,2,1,0:T(8,128)(2,1)S(1)}, bf16[1,1,64,128]{3,2,1,0:T(8,128)(2,1)S(1)}, u32[]{:S(2)}, u32[]{:S(2)}) collective-permute-start(bf16[1,1,64,128]{3,2,1,0:T(8,128)(2,1)S(1)} %get-tuple-element.19), channel_id=1, source_target_pairs={{0,8},{8,16},{16,24},{24,32},{32,40},{40,48},{48,56},{1,9},{9,17},... | collective-permute-start | bytes 49160 | tf_op jit(solution)/shard_map/ppermute | solution.py:31
  32.7 0.8 collective-permute-done
  33.5 0.8 select_maximum_fusion.4
  34.9 1.8 constant_dynamic-slice_fusion
  36.7 2.0 collective-permute-start.2
  39.0 1.4 collective-permute-start.4
  40.9 2.9 collective-permute-start.6
  44.7 1.0 collective-permute-start.7
  45.7 1.5 collective-permute-done.3
  47.3 2.6 collective-permute-start.8
  49.9 5.4 collective-permute-done.4
  55.3 8.7 %collective-permute-done.5 = bf16[3,3,128,128]{3,2,1,0:T(8,128)(2,1)S(1)} collective-permute-done((bf16[3,3,128,128]{3,2,1,0:T(8,128)(2,1)S(1)}, bf16[3,3,128,128]{3,2,1,0:T(8,128)(2,1)S(1)}, u32[]{:S(2)}, u32[]{:S(2)}) %collective-permute-start.5) | collective-permute-done | bytes 294944 | tf_op jit(solution)/shard_map/ppermute | solution.py:21
  64.1 6.5 collective-permute-done.6
  70.7 10.5 %collective-permute-done.8 = bf16[3,3,128,128]{3,2,1,0:T(8,128)(2,1)S(1)} collective-permute-done((bf16[3,3,128,128]{3,2,1,0:T(8,128)(2,1)S(1)}, bf16[3,3,128,128]{3,2,1,0:T(8,128)(2,1)S(1)}, u32[]{:S(2)}, u32[]{:S(2)}) %collective-permute-start.8) | collective-permute-done | bytes 294944 | tf_op jit(solution)/shard_map/ppermute | solution.py:21
  81.3 6.3 all-gather.6.cloned.1.call-done
  87.6 3.2 copy.56
  91.4 1.5 copy.33
  93.0 6.5 multiply_convert_fusion
  99.6 1.3 collective-permute-start.10
  100.9 8.7 %collective-permute-start.9 = (bf16[1,1,64,128]{3,2,1,0:T(8,128)(2,1)S(1)}, bf16[1,1,64,128]{3,2,1,0:T(8,128)(2,1)S(1)}, u32[]{:S(2)}, u32[]{:S(2)}) collective-permute-start(bf16[1,1,64,128]{3,2,1,0:T(8,128)(2,1)S(1)} %slice.123), channel_id=1, source_target_pairs={{0,8},{8,16},{16,24},{24,32},{32,40},{40,48},{48,56},{1,9},{9,17},... | collective-permute-start | bytes 49160 | tf_op jit(solution)/shard_map/ppermute | solution.py:31
  111.6 38.6 %all-gather.8.cloned.1.call-done = bf16[1,18,66,1024]{3,2,1,0:T(8,128)(2,1)} async-done(((bf16[1,18,66,128]{3,2,1,0:T(8,128)(2,1)}), bf16[1,18,66,1024]{3,2,1,0:T(8,128)(2,1)}) %all-gather.8.cloned.1.call-update) | async-done | bytes 2433040 | tf_op jit(solution)/shard_map/all_gather | solution.py:107
  150.2 3.2 copy.57
  153.9 1.5 copy.40
  155.6 5.7 fusion.81
  161.3 1.3 collective-permute-start.12
  162.7 8.0 %collective-permute-start.11 = (bf16[1,1,64,128]{3,2,1,0:T(8,128)(2,1)S(1)}, bf16[1,1,64,128]{3,2,1,0:T(8,128)(2,1)S(1)}, u32[]{:S(2)}, u32[]{:S(2)}) collective-permute-start(bf16[1,1,64,128]{3,2,1,0:T(8,128)(2,1)S(1)} %slice.129), channel_id=1, source_target_pairs={{0,8},{8,16},{16,24},{24,32},{32,40},{40,48},{48,56},{1,9},{9,17},... | collective-permute-start | bytes 49160 | tf_op jit(solution)/shard_map/ppermute | solution.py:31
  172.7 36.1 %all-gather.10.cloned.1.call-done = bf16[1,18,66,1024]{3,2,1,0:T(8,128)(2,1)} async-done(((bf16[1,18,66,128]{3,2,1,0:T(8,128)(2,1)}), bf16[1,18,66,1024]{3,2,1,0:T(8,128)(2,1)}) %all-gather.10.cloned.1.call-update) | async-done | bytes 2433040 | tf_op jit(solution)/shard_map/all_gather | solution.py:75
  208.8 3.2 copy.58
  212.5 1.5 copy.47
  214.2 7.3 %select_reduce_fusion.2 = (f32[128]{0:T(128)S(1)}, f32[128]{0:T(128)S(1)}, f32[]{:T(128)}, f32[16,8,9,128]{3,1,2,0:T(8,128)}) fusion(pred[8,9]{0,1:T(8,128)(4,1)S(1)} %copy-done.15, f32[16,8,9,128]{3,1,2,0:T(8,128)S(1)} %copy-done.13, f32[128]{0:T(128)S(1)} %convolution_bitcast_fusion.9, ...), kind=kOutput, calls=%fused_computation.90 | convolution fusion | flops 2730147840 | bytes 6710860 | tf_op jit(solution)/shard_map/conv_general_dilated | solution.py:40
  222.3 201.7 %psum.21 = f32[1]{0:T(128)} all-reduce(f32[1]{0:T(128)} %bitcast.10), channel_id=1, replica_groups=mesh['dp'=4,'space'=8,'tensor'=8] {'space','tensor'}, use_global_device_ids=true, to_apply=%region_1.2 | all-reduce | flops 1 | bytes 8 | tf_op jit(solution)/shard_map/psum | solution.py:102
  424.7 1.7 fusion.91
  427.6 1.8 convolution_bitcast_fusion.4
  429.4 1.8 convolution_bitcast_fusion.1
  431.2 0.8 convolution_bitcast_fusion
  433.0 1.6 copy-done.7
  437.0 0.8 convolution_bitcast_fusion.3
  438.7 1.9 maximum_bitcast_fusion.3
  440.6 1.0 broadcast_multiply_fusion
  441.6 16.8 %all-gather.12.cloned.1.call-done = bf16[16,1,64,1024]{3,2,0,1:T(8,128)(2,1)} async-done(((bf16[16,1,64,128]{3,2,0,1:T(8,128)(2,1)}), bf16[16,1,64,1024]{3,2,0,1:T(8,128)(2,1)}) %all-gather.12.cloned.1.call-update) | async-done | bytes 2097168 | tf_op jit(solution)/shard_map/all_gather | solution.py:116
  458.4 2.2 fusion.69
  464.9 1.1 copy-done.4
  466.5 2.7 maximum_add_fusion
  469.2 173.2 %all-reduce.6.cloned.1.call-done = (f32[3,3,128,1024]{3,2,1,0:T(8,128)}, f32[1000,128]{1,0:T(8,128)}) async-done(((f32[3,3,128,1024]{3,2,1,0:T(8,128)}, f32[1000,128]{1,0:T(8,128)}), (f32[3,3,128,1024]{3,2,1,0:T(8,128)}, f32[1000,128]{1,0:T(8,128)})) %all-reduce.6.cloned.1.call-update) | async-done | bytes 5230608 | tf_op jit(solution)/shard_map/psum | solution.py:122
  642.4 5.3 copy.78
  (115 shorter events, 20.0 us)
Async XLA Ops:
  7.2 37.3 %copy-start = (f32[1000,128]{1,0:T(8,128)S(1)}, f32[1000,128]{1,0:T(8,128)}, u32[]{:S(2)}) copy-start(f32[1000,128]{1,0:T(8,128)} %param.6) | copy-start | bytes 1536004
  7.2 80.4 %all-gather.6.cloned.1.call-start = ((), (), s32[]{:S(2)}) async-start(), calls=%async_computation.1 | async-start | bytes 2985984 | tf_op jit(solution)/shard_map/all_gather | solution.py:75
  21.9 10.8 %collective-permute-start.1 = (bf16[1,1,64,128]{3,2,1,0:T(8,128)(2,1)S(1)}, bf16[1,1,64,128]{3,2,1,0:T(8,128)(2,1)S(1)}, u32[]{:S(2)}, u32[]{:S(2)}) collective-permute-start(bf16[1,1,64,128]{3,2,1,0:T(8,128)(2,1)S(1)} %get-tuple-element.20), channel_id=1, source_target_pairs={{8,0},{16,8},{24,16},{32,24},{40,32},{48,40},{56,48},{9,1},{17,9},... | collective-permute-start | bytes 49160 | tf_op jit(solution)/shard_map/ppermute | solution.py:34
  23.2 10.3 %collective-permute-start = (bf16[1,1,64,128]{3,2,1,0:T(8,128)(2,1)S(1)}, bf16[1,1,64,128]{3,2,1,0:T(8,128)(2,1)S(1)}, u32[]{:S(2)}, u32[]{:S(2)}) collective-permute-start(bf16[1,1,64,128]{3,2,1,0:T(8,128)(2,1)S(1)} %get-tuple-element.19), channel_id=1, source_target_pairs={{0,8},{8,16},{16,24},{24,32},{32,40},{40,48},{48,56},{1,9},{9,17},... | collective-permute-start | bytes 49160 | tf_op jit(solution)/shard_map/ppermute | solution.py:31
  34.4 115.8 %all-gather.8.cloned.1.call-start = ((), (), s32[]{:S(2)}) async-start(), calls=%async_computation.2 | async-start | bytes 2985984 | tf_op jit(solution)/shard_map/all_gather | solution.py:107
  36.7 8.0 %collective-permute-start.2 = (bf16[3,3,128,128]{3,2,1,0:T(8,128)(2,1)S(1)}, bf16[3,3,128,128]{3,2,1,0:T(8,128)(2,1)S(1)}, u32[]{:S(2)}, u32[]{:S(2)}) collective-permute-start(bf16[3,3,128,128]{3,2,1,0:T(8,128)(2,1)S(1)} %get-tuple-element.13), channel_id=1, source_target_pairs={{0,1},{1,0},{2,3},{3,2},{4,5},{5,4},{6,7},{7,6},{8,9},{9,8},{10,11... | collective-permute-start | bytes 884744 | tf_op jit(solution)/shard_map/ppermute | solution.py:21
  38.7 8.6 %collective-permute-start.3 = (bf16[3,3,128,128]{3,2,1,0:T(8,128)(2,1)S(1)}, bf16[3,3,128,128]{3,2,1,0:T(8,128)(2,1)S(1)}, u32[]{:S(2)}, u32[]{:S(2)}) collective-permute-start(bf16[3,3,128,128]{3,2,1,0:T(8,128)(2,1)S(1)} %get-tuple-element.12), channel_id=1, source_target_pairs={{0,2},{1,3},{2,0},{3,1},{4,6},{5,7},{6,4},{7,5},{8,10},{9,11},{10,... | collective-permute-start | bytes 884744 | tf_op jit(solution)/shard_map/ppermute | solution.py:21
  39.0 16.3 %collective-permute-start.4 = (bf16[3,3,128,128]{3,2,1,0:T(8,128)(2,1)S(1)}, bf16[3,3,128,128]{3,2,1,0:T(8,128)(2,1)S(1)}, u32[]{:S(2)}, u32[]{:S(2)}) collective-permute-start(bf16[3,3,128,128]{3,2,1,0:T(8,128)(2,1)S(1)} %get-tuple-element.11), channel_id=1, source_target_pairs={{0,3},{1,2},{2,1},{3,0},{4,7},{5,6},{6,5},{7,4},{8,11},{9,10},{10,... | collective-permute-start | bytes 884744 | tf_op jit(solution)/shard_map/ppermute | solution.py:21
  40.4 23.6 %collective-permute-start.5 = (bf16[3,3,128,128]{3,2,1,0:T(8,128)(2,1)S(1)}, bf16[3,3,128,128]{3,2,1,0:T(8,128)(2,1)S(1)}, u32[]{:S(2)}, u32[]{:S(2)}) collective-permute-start(bf16[3,3,128,128]{3,2,1,0:T(8,128)(2,1)S(1)} %get-tuple-element.10), channel_id=1, source_target_pairs={{0,4},{1,5},{2,6},{3,7},{4,0},{5,1},{6,2},{7,3},{8,12},{9,13},{10,... | collective-permute-start | bytes 884744 | tf_op jit(solution)/shard_map/ppermute | solution.py:21
  40.9 29.8 %collective-permute-start.6 = (bf16[3,3,128,128]{3,2,1,0:T(8,128)(2,1)S(1)}, bf16[3,3,128,128]{3,2,1,0:T(8,128)(2,1)S(1)}, u32[]{:S(2)}, u32[]{:S(2)}) collective-permute-start(bf16[3,3,128,128]{3,2,1,0:T(8,128)(2,1)S(1)} %get-tuple-element.9), channel_id=1, source_target_pairs={{0,5},{1,4},{2,7},{3,6},{4,1},{5,0},{6,3},{7,2},{8,13},{9,12},{10,... | collective-permute-start | bytes 884744 | tf_op jit(solution)/shard_map/ppermute | solution.py:21
  44.7 26.0 %collective-permute-start.7 = (bf16[3,3,128,128]{3,2,1,0:T(8,128)(2,1)S(1)}, bf16[3,3,128,128]{3,2,1,0:T(8,128)(2,1)S(1)}, u32[]{:S(2)}, u32[]{:S(2)}) collective-permute-start(bf16[3,3,128,128]{3,2,1,0:T(8,128)(2,1)S(1)} %get-tuple-element.8), channel_id=1, source_target_pairs={{0,6},{1,7},{2,4},{3,5},{4,2},{5,3},{6,0},{7,1},{8,14},{9,15},{10,... | collective-permute-start | bytes 884744 | tf_op jit(solution)/shard_map/ppermute | solution.py:21
  47.3 34.0 %collective-permute-start.8 = (bf16[3,3,128,128]{3,2,1,0:T(8,128)(2,1)S(1)}, bf16[3,3,128,128]{3,2,1,0:T(8,128)(2,1)S(1)}, u32[]{:S(2)}, u32[]{:S(2)}) collective-permute-start(bf16[3,3,128,128]{3,2,1,0:T(8,128)(2,1)S(1)} %get-tuple-element.7), channel_id=1, source_target_pairs={{0,7},{1,6},{2,5},{3,4},{4,3},{5,2},{6,1},{7,0},{8,15},{9,14},{10,... | collective-permute-start | bytes 884744 | tf_op jit(solution)/shard_map/ppermute | solution.py:21
  91.4 1.6 copy-start.15
  99.6 10.2 %collective-permute-start.10 = (bf16[1,1,64,128]{3,2,1,0:T(8,128)(2,1)S(1)}, bf16[1,1,64,128]{3,2,1,0:T(8,128)(2,1)S(1)}, u32[]{:S(2)}, u32[]{:S(2)}) collective-permute-start(bf16[1,1,64,128]{3,2,1,0:T(8,128)(2,1)S(1)} %slice.126), channel_id=1, source_target_pairs={{8,0},{16,8},{24,16},{32,24},{40,32},{48,40},{56,48},{9,1},{17,9},... | collective-permute-start | bytes 49160 | tf_op jit(solution)/shard_map/ppermute | solution.py:34
  100.9 9.5 %collective-permute-start.9 = (bf16[1,1,64,128]{3,2,1,0:T(8,128)(2,1)S(1)}, bf16[1,1,64,128]{3,2,1,0:T(8,128)(2,1)S(1)}, u32[]{:S(2)}, u32[]{:S(2)}) collective-permute-start(bf16[1,1,64,128]{3,2,1,0:T(8,128)(2,1)S(1)} %slice.123), channel_id=1, source_target_pairs={{0,8},{8,16},{16,24},{24,32},{32,40},{40,48},{48,56},{1,9},{9,17},... | collective-permute-start | bytes 49160 | tf_op jit(solution)/shard_map/ppermute | solution.py:31
  111.3 97.4 %all-gather.10.cloned.1.call-start = ((), (), s32[]{:S(2)}) async-start(), calls=%async_computation.3 | async-start | bytes 2985984 | tf_op jit(solution)/shard_map/all_gather | solution.py:75
  153.9 1.7 copy-start.8
  161.3 10.2 %collective-permute-start.12 = (bf16[1,1,64,128]{3,2,1,0:T(8,128)(2,1)S(1)}, bf16[1,1,64,128]{3,2,1,0:T(8,128)(2,1)S(1)}, u32[]{:S(2)}, u32[]{:S(2)}) collective-permute-start(bf16[1,1,64,128]{3,2,1,0:T(8,128)(2,1)S(1)} %slice.132), channel_id=1, source_target_pairs={{8,0},{16,8},{24,16},{32,24},{40,32},{48,40},{56,48},{9,1},{17,9},... | collective-permute-start | bytes 49160 | tf_op jit(solution)/shard_map/ppermute | solution.py:34
  162.7 8.9 %collective-permute-start.11 = (bf16[1,1,64,128]{3,2,1,0:T(8,128)(2,1)S(1)}, bf16[1,1,64,128]{3,2,1,0:T(8,128)(2,1)S(1)}, u32[]{:S(2)}, u32[]{:S(2)}) collective-permute-start(bf16[1,1,64,128]{3,2,1,0:T(8,128)(2,1)S(1)} %slice.129), channel_id=1, source_target_pairs={{0,8},{8,16},{16,24},{24,32},{32,40},{40,48},{48,56},{1,9},{9,17},... | collective-permute-start | bytes 49160 | tf_op jit(solution)/shard_map/ppermute | solution.py:31
  170.8 0.7 copy-start.12
  171.5 40.4 %copy-start.10 = (bf16[16,1,64,128]{3,2,0,1:T(8,128)(2,1)}, bf16[16,1,64,128]{3,2,0,1:T(8,128)(2,1)S(1)}, u32[]{:S(2)}) copy-start(bf16[16,1,64,128]{3,2,0,1:T(8,128)(2,1)S(1)} %copy.66) | copy-start | bytes 786436
  172.4 285.9 %all-gather.12.cloned.1.call-start = ((), (), s32[]{:S(2)}) async-start(), calls=%async_computation.4 | async-start | bytes 2359296 | tf_op jit(solution)/shard_map/all_gather | solution.py:116
  212.5 1.6 copy-start.13
  221.4 206.1 %copy-start.6 = (bf16[1,18,66,1024]{3,2,1,0:T(8,128)(2,1)S(1)}, bf16[1,18,66,1024]{3,2,1,0:T(8,128)(2,1)}, u32[]{:S(2)}) copy-start(bf16[1,18,66,1024]{3,2,1,0:T(8,128)(2,1)} %all-gather.8.cloned.1.call-done) | copy-start | bytes 7299076
  427.3 215.1 %all-reduce.6.cloned.1.call-start = ((), (), s32[]{:S(2)}) async-start(), calls=%async_computation.5 | async-start | bytes 10461184 | tf_op jit(solution)/shard_map/psum | solution.py:122
  429.4 1.8 copy-start.9
  432.8 1.8 copy-start.7
  432.8 1.7 copy-start.11
  438.6 19.7 %copy-start.3 = (bf16[1,18,66,128]{3,2,1,0:T(8,128)(2,1)S(1)}, bf16[1,18,66,128]{3,2,1,0:T(8,128)(2,1)}, u32[]{:S(2)}) copy-start(bf16[1,18,66,128]{3,2,1,0:T(8,128)(2,1)} %select_maximum_fusion.4) | copy-start | bytes 912388
  458.3 2.2 copy-start.2
  464.6 1.4 copy-start.4
  464.6 1.9 copy-start.5
  642.4 5.3 copy-start.14
  642.4 6.1 copy-start.1
Sparse Core Ops, SparseCore 0:
  34.5 53.0 all-gather.5
  111.5 38.6 all-gather.7
  172.6 36.1 all-gather.9
  427.4 30.9 all-gather.11
  469.3 173.0 all-reduce.5
